TPU v7x, 32 devices: a whole 2x2x4 slice. The times are simulated.
32 devices in a mesh: gy: 4 (over z), gx: 8 (over y, x, core).
Axes of the slice: x: 2, y: 2, z: 4, core: 2. Of those that a mesh axis runs over, the one named last changes fastest.
Arguments:
- positions: float32 [3, 8, 32768], P(None, 'gx', 'gy'), may hold values from -6 to 6
- velocities: float32 [3, 8, 32768], P(None, 'gx', 'gy'), may hold values from -6 to 6
- radius: float32 [8, 32768], P('gx', 'gy'), may hold values from 0.6 to 1
- sphere_cell: int32 [8, 32768], P('gx', 'gy'), may hold values from -1 to 8191, as said below
- pair_route: int32 [8, 256, 1], P('gx', 'gy'), may hold values from 0 to 6; in each aligned block of 64 rows (0 to 63, 64 to 127, ..., all dimensions but the last counted through in order) at most 16 rows name the same one
- pair_mine: int32 [8, 256], P('gx', 'gy'), may hold values from 0 to 63
- pair_theirs: int32 [8, 256], P('gx', 'gy'), may hold values from 0 to 63
- brick_owner: int32 [8, 4], P('gx'), may hold values from 0 to 3, each once within a row
- fluid_velocity: float32 [3, 8, 8192], P(None, 'gx', 'gy'), may hold values from -6 to 6
- pressure_grad: float32 [3, 8, 8192], P(None, 'gx', 'gy'), may hold values from -6 to 6
Outputs:
- new_velocity: float32 [3, 8, 32768], P(None, 'gx', 'gy')
- drag_source: float32 [3, 8, 8192], P(None, 'gx', 'gy')
Inputs may be any that keep to these rules, and one draw needn't show every extreme that they name: `pair_route`: the pairs of one device name one offset at most 16 times, a bound that some block reaches. `sphere_cell`: in every block of 128 slots the live slots come first and are half of the block or more; every device has a full block.
All inputs are finite; a program needn't handle non-finite values.
Results may differ from a plain program's by a relative error of at most 0.0003.
Values sent between devices are 32-bit elements; how exact they have to be, the bound alone decides.
A program may use at most 128 MiB of HBM per device.

v0:
```python
import math

import jax
import jax.numpy as jnp
from jax import lax
from jax.sharding import PartitionSpec as P

stiffness = 0.05
damping = 0.02
drag_coeff = 0.5
time_step = 0.2


def contact(left_state, right_state):
    offset = left_state[:, 0:3, :, None] - right_state[:, 0:3, None, :]
    dist_sq = (
        offset[:, 0] * offset[:, 0] + offset[:, 1] * offset[:, 1] + offset[:, 2] * offset[:, 2]
    )
    radius_sum = left_state[:, 6, :, None] + right_state[:, 6, None, :]
    weight = jnp.exp(-dist_sq / (2.0 * radius_sum * radius_sum)) * (
        left_state[:, 7, :, None] * right_state[:, 7, None, :]
    )
    relative = left_state[:, 3:6, :, None] - right_state[:, 3:6, None, :]
    pulling = weight[:, None] * (stiffness * offset - damping * relative)
    return (jnp.sum(pulling, axis=3), -jnp.sum(pulling, axis=2))


def contact_pair(pair_in):
    return contact(pair_in[0], pair_in[1])


def grouped(left_all, right_all):
    count_all = left_all.shape[0]
    width = left_all.shape[2]
    group_size = math.gcd(count_all, 8)
    shaped = (
        left_all.reshape(count_all // group_size, group_size, 8, width),
        right_all.reshape(count_all // group_size, group_size, 8, width),
    )
    on_left, on_right = lax.map(contact_pair, shaped)
    return (on_left.reshape(count_all, 3, width), on_right.reshape(count_all, 3, width))


def on_device(
    positions,
    velocities,
    radius,
    sphere_cell,
    pair_route,
    pair_mine,
    pair_theirs,
    brick_owner,
    fluid_velocity,
    pressure_grad,
):
    width = 128
    sphere_total = positions.shape[2]
    blocks = sphere_total // width
    alive_mask = (sphere_cell[0] >= 0).astype(jnp.float32)
    states = jnp.concatenate(
        [positions[:, 0], velocities[:, 0], radius[0][None], alive_mask[None]], axis=0
    )
    states = states.reshape(8, blocks, width).transpose(1, 0, 2)
    gy_count = lax.axis_size("gy")
    cells_dev = fluid_velocity.shape[2]
    column_u, column_p = (
        lax.all_gather(fluid_velocity, "gy", axis=2, tiled=True),
        lax.all_gather(pressure_grad, "gy", axis=2, tiled=True),
    )
    gx_count = lax.axis_size("gx")
    my_index = lax.axis_index("gx")
    pair_total = pair_route.shape[1]
    capacity = max(2, 2 * pair_total // gx_count)
    slot_total = gx_count * capacity
    target = (my_index + 1 + pair_route[0, :, 0]) % gx_count
    onehot_target = (target[:, None] == jnp.arange(gx_count, dtype=jnp.int32)[None, :]).astype(
        jnp.int32
    )
    order_in = jnp.sum(jnp.cumsum(onehot_target, axis=0) * onehot_target, axis=1) - 1
    slot_index = target * capacity + order_in
    wanted = jnp.full((slot_total,), -1, jnp.int32).at[slot_index].set(pair_theirs[0])
    owned_block = jnp.zeros((slot_total,), jnp.int32).at[slot_index].set(pair_mine[0])
    asked = lax.all_to_all(
        wanted.reshape(gx_count, capacity), "gx", split_axis=0, concat_axis=0, tiled=True
    )
    valid_ask = (asked >= 0).astype(jnp.float32)
    served = states[jnp.clip(asked, 0, blocks - 1)] * valid_ask[:, :, None, None]
    partner = lax.all_to_all(served, "gx", split_axis=0, concat_axis=0, tiled=True)
    own_slots = states[owned_block].reshape(gx_count, capacity, 8, width)
    beside = jnp.concatenate([states[1:], jnp.zeros_like(states[:1])], axis=0)
    self_force, unused_self = grouped(states, states)
    near_force, back_force = grouped(states, beside)
    local_force = (
        self_force
        + near_force
        + jnp.concatenate([jnp.zeros_like(back_force[:1]), back_force[:-1]], axis=0)
    )
    on_owner, on_partner = grouped(
        own_slots.reshape(slot_total, 8, width), partner.reshape(slot_total, 8, width)
    )
    returned = lax.all_to_all(
        on_partner.reshape(gx_count, capacity, 3, width),
        "gx",
        split_axis=0,
        concat_axis=0,
        tiled=True,
    )
    block_ids = jnp.arange(blocks, dtype=jnp.int32)[:, None]
    owner_hot = (owned_block[None, :] == block_ids).astype(jnp.float32)
    served_hot = (asked.reshape(-1)[None, :] == block_ids).astype(jnp.float32)
    remote_force = jnp.dot(
        owner_hot,
        on_owner.reshape(slot_total, 3 * width),
        precision=lax.Precision.HIGHEST,
        preferred_element_type=jnp.float32,
    )
    remote_force = remote_force + jnp.dot(
        served_hot,
        returned.reshape(slot_total, 3 * width),
        precision=lax.Precision.HIGHEST,
        preferred_element_type=jnp.float32,
    )
    total_force = local_force + remote_force.reshape(blocks, 3, width)
    contact_force = total_force.transpose(1, 0, 2).reshape(3, sphere_total)
    cell_here = sphere_cell[0]
    block_of = cell_here // cells_dev
    within = cell_here % cells_dev
    owner_of = jnp.sum(
        jnp.where(
            block_of[:, None] == jnp.arange(gy_count, dtype=jnp.int32)[None, :],
            brick_owner[0][None, :],
            0,
        ),
        axis=1,
    )
    storage = jnp.where(cell_here >= 0, owner_of * cells_dev + within, 0)
    fluid_at = jnp.take(column_u[:, 0], storage, axis=1)
    grad_at = jnp.take(column_p[:, 0], storage, axis=1)
    speed = velocities[:, 0]
    radii = radius[0]
    sphere_cube = radii * radii * radii
    drag_force = alive_mask * drag_coeff * radii * (fluid_at - speed)
    fluid_force = drag_force - alive_mask * sphere_cube * grad_at
    new_velocity = speed + time_step * (contact_force + fluid_force) / sphere_cube
    deposit = jax.ops.segment_sum(-drag_force.T, storage, num_segments=gy_count * cells_dev)
    drag_source = lax.psum_scatter(
        deposit.T.reshape(3, 1, gy_count * cells_dev), "gy", scatter_dimension=2, tiled=True
    )
    return (new_velocity.reshape(3, 1, sphere_total), drag_source)


def solution(mesh):
    placed = (
        P(None, "gx", "gy"),
        P(None, "gx", "gy"),
        P("gx", "gy"),
        P("gx", "gy"),
        P("gx", "gy", None),
        P("gx", "gy"),
        P("gx", "gy"),
        P("gx", None),
        P(None, "gx", "gy"),
        P(None, "gx", "gy"),
    )
    return jax.shard_map(
        on_device,
        mesh=mesh,
        in_specs=placed,
        out_specs=(P(None, "gx", "gy"), P(None, "gx", "gy")),
        check_vma=False,
    )
```

profile of v0, /device:TPU:0, one launch (start us, length us, event | category | flops | bytes accessed | tf_op | source)
XLA Modules:
  0.0 433.3 jit_solution(1129177580165425845)
XLA Ops:
  7.2 0.7 and_select_fusion.1
  8.2 0.7 fusion.59
  8.9 0.9 scatter_custom_fusion.1
  9.8 0.7 all_to_all.12
  10.4 5.2 %all-to-all-start = ((s32[8,1,16]{2,1,0:T(1,128)}), s32[8,1,16]{2,1,0:T(1,128)S(1)}, u32[]{:S(2)}, u32[]{:S(2)}) async-start(s32[8,1,16]{2,1,0:T(1,128)} %bitcast.43), calls=%async_computation | async-start | bytes 8192 | tf_op jit(solution)/shard_map/all_to_all | solution.py:83
  15.7 0.8 add_select_fusion.1
  16.4 0.8 select_reduce_fusion
  17.3 0.8 compare_and_fusion
  18.1 1.1 copy.74
  19.2 73.0 %all_gather.6 = f32[3,1,8192]{0,2,1:T(8,128)} all-gather(f32[3,1,2048]{0,2,1:T(8,128)S(1)} %copy.74), channel_id=1, replica_groups=mesh['gy'=4,'gx'=8] {'gy'}, dimensions={2}, use_global_device_ids=true | all-gather | bytes 122880 | tf_op jit(solution)/shard_map/all_gather | solution.py:67
  92.3 2.7 copy.62
  95.1 29.9 %gather_fusion.2 = f32[8192,3]{1,0:T(8,128)} fusion(f32[3,8192]{0,1:T(8,128)} %bitcast.188, s32[8192]{0:T(1024)S(1)} %broadcast_clamp_fusion), kind=kCustom, calls=%fused_computation.clone | custom fusion | bytes 229376 | tf_op jit(solution)/shard_map/jit(_take)/gather | solution.py:137
  124.9 54.5 %scatter_custom_fusion.2 = f32[8192,3]{1,0:T(8,128)} fusion(s32[8192]{0:T(1024)S(1)} %bitcast.222, f32[3,1,8192]{0,2,1:T(8,128)} %copy.62, f32[8192,3]{1,0:T(8,128)} %gather_fusion.2, f32[]{:T(128)} %constant.137.clone.2, f32[]{:T(128)} %constant.139.clone.1, f32[8192]{0:T(1024)S(1)} %bitcast.211, pred[8192]{0:T(1024)(128)(4,1)S(1)} %get-tuple-element.133), kind=kCustom, calls=%fused_computation.60 | custom fusion | flops 122880 | bytes 335880 | tf_op jit(solution)/shard_map/scatter-add | solution.py:145
  179.5 0.8 copy-done.3
  180.8 20.6 %while.36 = (s32[]{:T(128)}, f32[8,8,3,128]{3,2,1,0:T(4,128)S(1)}, f32[8,8,3,128]{3,2,1,0:T(4,128)S(1)}, f32[8,8,8,128]{3,2,1,0:T(8,128)S(1)}, f32[8,8,8,128]{3,2,1,0:T(8,128)S(1)}, /*index=5*/s32[]{:T(128)}) while((s32[]{:T(128)}, f32[8,8,3,128]{3,2,1,0:T(4,128)S(1)}, f32[8,8,3,128]{3,2,1,0:T(4,128)S(1)}, f32[8,8,8,128]{3,2,1,0:T(8,128)S(1)}, ...), condition=%wide.region_6.7_spmd, body=%wide.region_3.6_spmd.sunk | while | flops 5108738 | bytes 4636753 | solution.py:40
  181.8 1.6 fusion.98
  184.4 1.6 fusion.98
  186.9 1.6 fusion.98
  189.5 1.6 fusion.98
  192.1 1.6 fusion.98
  194.7 1.6 fusion.98
  197.2 1.6 fusion.98
  199.8 1.6 fusion.98
  201.6 0.8 gather_fusion.1
  202.3 1.0 broadcast_multiply_fusion
  203.3 4.1 all-to-all-start.1
  207.5 19.1 %while.35 = (s32[]{:T(128)}, f32[8,8,3,128]{3,2,1,0:T(4,128)S(1)}, f32[8,8,8,128]{3,2,1,0:T(8,128)S(1)}, s32[]{:T(128)}) while((s32[]{:T(128)}, f32[8,8,3,128]{3,2,1,0:T(4,128)S(1)}, f32[8,8,8,128]{3,2,1,0:T(8,128)S(1)}, s32[]{:T(128)}) %tuple.114), condition=%wide.region_2.3_spmd, body=%wide.region_0.2_spmd.sunk | while | flops 4715522 | bytes 4423741 | solution.py:40
  208.4 1.5 multiply_reduce_fusion.2
  210.8 1.5 multiply_reduce_fusion.2
  213.2 1.5 multiply_reduce_fusion.2
  215.6 1.5 multiply_reduce_fusion.2
  218.0 1.5 multiply_reduce_fusion.2
  220.4 1.5 multiply_reduce_fusion.2
  222.8 1.5 multiply_reduce_fusion.2
  225.1 1.5 multiply_reduce_fusion.2
  226.7 0.9 scatter_custom_fusion
  227.6 0.8 gather_fusion
  228.8 96.0 %all_gather.7 = f32[3,1,8192]{0,2,1:T(8,128)} all-gather(f32[3,1,2048]{0,2,1:T(8,128)S(1)} %copy.75), channel_id=1, replica_groups=mesh['gy'=4,'gx'=8] {'gy'}, dimensions={2}, use_global_device_ids=true | all-gather | bytes 122880 | tf_op jit(solution)/shard_map/all_gather | solution.py:68
  324.7 29.9 %gather_fusion.3 = f32[8192,3]{1,0:T(8,128)} fusion(f32[3,8192]{0,1:T(8,128)} %bitcast.189, s32[8192]{0:T(1024)S(1)} %broadcast_clamp_fusion), kind=kCustom, calls=%fused_computation.1.clone | custom fusion | bytes 229376 | tf_op jit(solution)/shard_map/jit(_take)/gather | solution.py:138
  355.2 0.7 reduce.3
  355.9 2.2 copy.77
  358.1 41.1 %while.37 = (s32[]{:T(128)}, f32[16,8,3,128]{3,2,1,0:T(4,128)S(1)}, f32[16,8,3,128]{3,2,1,0:T(4,128)S(1)}, f32[16,8,8,128]{3,2,1,0:T(8,128)S(1)}, f32[16,8,8,128]{3,2,1,0:T(8,128)S(1)}, /*index=5*/s32[]{:T(128)}) while((s32[]{:T(128)}, f32[16,8,3,128]{3,2,1,0:T(4,128)S(1)}, f32[16,8,3,128]{3,2,1,0:T(4,128)S(1)}, ...), condition=%wide.region_14.15_spmd, body=%wide.region_11.14_spmd.sunk | while | flops 5108738 | bytes 4636753 | solution.py:40
  359.0 1.6 fusion.104
  361.6 1.6 fusion.104
  364.1 1.6 fusion.104
  366.7 1.6 fusion.104
  369.3 1.6 fusion.104
  371.9 1.6 fusion.104
  374.4 1.6 fusion.104
  377.0 1.6 fusion.104
  379.6 1.6 fusion.104
  382.1 1.6 fusion.104
  384.7 1.6 fusion.104
  387.3 1.6 fusion.104
  389.8 1.6 fusion.104
  392.4 1.6 fusion.104
  395.0 1.6 fusion.104
  397.6 1.6 fusion.104
  399.2 0.7 copy.71
  399.9 3.7 all-to-all-start.2
  403.8 6.0 %all-to-all-done.2 = f32[8,16,3,128]{3,1,2,0:T(8,128)S(1)} async-done(((f32[8,16,3,128]{3,1,2,0:T(8,128)}), f32[8,16,3,128]{3,1,2,0:T(8,128)S(1)}, u32[]{:S(2)}, u32[]{:S(2)}) %all-to-all-start.2) | async-done | bytes 196640 | tf_op jit(solution)/shard_map/all_to_all | solution.py:101
  410.2 2.7 copy.73
  412.9 10.1 %fusion.32 = f32[3,1,8192]{0,2,1:T(8,128)} fusion(f32[3,64,128]{0,2,1:T(8,128)} %copy.73, f32[3,1,8192]{0,2,1:T(8,128)} %copy.62, f32[8192,3]{1,0:T(8,128)} %gather_fusion.3, f32[8192,3]{1,0:T(8,128)} %gather_fusion.2, f32[8192]{0:T(1024)S(1)} %bitcast.217, f32[8192]{0:T(1024)S(1)} %bitcast.216, f32[8192]{0:T(1024)S(1)} %bitcast.212, ...), kind=kLoop, calls=%fused_computation.68 | loop fusion | flops 245760 | bytes 598016 | tf_op jit(solution)/shard_map/reshape | solution.py:149
  423.0 3.5 copy.76
  (313 shorter events, 31.5 us)
Async XLA Ops:
  10.4 191.0 %all-to-all-start = ((s32[8,1,16]{2,1,0:T(1,128)}), s32[8,1,16]{2,1,0:T(1,128)S(1)}, u32[]{:S(2)}, u32[]{:S(2)}) async-start(s32[8,1,16]{2,1,0:T(1,128)} %bitcast.43), calls=%async_computation | async-start | bytes 8192 | tf_op jit(solution)/shard_map/all_to_all | solution.py:83
  15.6 340.3 %reduce-scatter.2.cloned.1.call-start = ((), (), s32[]{:S(2)}) async-start(), calls=%async_computation.4 | async-start | bytes 5242880 | tf_op jit(solution)/shard_map/reduce_scatter | solution.py:146
  19.2 73.0 %copy-start = (s32[1,8192]{1,0:T(1,128)S(1)}, s32[1,8192]{1,0:T(1,128)}, u32[]{:S(2)}) copy-start(s32[1,8192]{1,0:T(1,128)} %param.21) | copy-start | bytes 98308
  19.2 73.0 %copy-start.2 = (f32[1,8192]{1,0:T(1,128)S(1)}, f32[1,8192]{1,0:T(1,128)}, u32[]{:S(2)}) copy-start(f32[1,8192]{1,0:T(1,128)} %param.20) | copy-start | bytes 98308
  19.2 73.0 %copy-start.1 = (f32[3,1,8192]{2,1,0:T(1,128)S(1)}, f32[3,1,8192]{2,1,0:T(1,128)}, u32[]{:S(2)}) copy-start(f32[3,1,8192]{2,1,0:T(1,128)} %param.19) | copy-start | bytes 294916
  179.4 0.9 copy-start.3
  203.3 154.8 %all-to-all-start.1 = ((f32[8,16,8,128]{3,2,1,0:T(8,128)}), f32[8,16,8,128]{3,2,1,0:T(8,128)S(1)}, u32[]{:S(2)}, u32[]{:S(2)}) async-start(f32[8,16,8,128]{3,2,1,0:T(8,128)} %broadcast_multiply_fusion), calls=%async_computation.1 | async-start | bytes 1048576 | tf_op jit(solution)/shard_map/all_to_all | solution.py:88
  207.5 20.9 %copy-start.4 = (f32[3,1,2048]{2,1,0:T(1,128)S(1)}, f32[3,1,2048]{2,1,0:T(1,128)}, u32[]{:S(2)}) copy-start(f32[3,1,2048]{2,1,0:T(1,128)} %param.27) | copy-start | bytes 73732
  399.9 9.9 %all-to-all-start.2 = ((f32[8,16,3,128]{3,1,2,0:T(8,128)}), f32[8,16,3,128]{3,1,2,0:T(8,128)S(1)}, u32[]{:S(2)}, u32[]{:S(2)}) async-start(f32[8,16,3,128]{3,1,2,0:T(8,128)} %copy.71), calls=%async_computation.2 | async-start | bytes 393216 | tf_op jit(solution)/shard_map/all_to_all | solution.py:101
Sparse Core Ops, SparseCore 0:
  179.6 102.1 reduce-scatter.1
where the time goes:
time: 434 us; the launch traced here: 433 us
  blocking collectives  169 us (39%)
  other arithmetic  147 us (34%)
  local copies, waits for them, and re-layouts  80.6 us (19%)
  between operations  14.4 us (3%)
  starting transfers between devices  13 us (3%)
  waiting for transfers between devices  6.04 us (1%)
    all_gather x1, blocking collectives, on_device(): lax.all_gather(pressure_grad, 'gy', axis=2, tiled=True)  96 us
    all_gather x1, blocking collectives, on_device(): lax.all_gather(fluid_velocity, 'gy', axis=2, tiled=True)  73 us
    scatter-add x1, other arithmetic, on_device(): jax.ops.segment_sum(-drag_force.T, storage, num_segments=gy_count * cells...  54.5 us
    reduce_sum x32, other arithmetic, contact(): return (jnp.sum(pulling, axis=3), -jnp.sum(pulling, axis=2))  49.8 us
    gather x1, local copies, waits for them, and re-layouts, on_device(): grad_at = jnp.take(column_p[:, 0], storage, axis=1)  29.9 us
    gather x1, local copies, waits for them, and re-layouts, on_device(): fluid_at = jnp.take(column_u[:, 0], storage, axis=1)  29.9 us
    sub x32, other arithmetic, contact(): offset = left_state[:, 0:3, :, None] - right_state[:, 0:3, None, :]  14.9 us
    mul x32, other arithmetic, contact(): pulling = weight[:, None] * (stiffness * offset - damping * relative)  11.5 us
  transfers between devices with their start and end apart: 4, of which 1 were waited for; matrix products, arithmetic and copies ran while one was open for 39% of the time, Pallas kernels for 0%

commit v1 on v0

v1 whole, which is shorter than its diff:
```python
import functools
import math

import jax
import jax.numpy as jnp
from jax import lax
from jax.experimental import pallas as pl
from jax.experimental.pallas import tpu as pltpu
from jax.sharding import PartitionSpec as P

stiffness = 0.05
damping = 0.02
drag_coeff = 0.5
time_step = 0.2
WIDTH = 128
NT = (((1,), (1,)), ((), ()))
NN = (((1,), (0,)), ((), ()))
VMEM = pl.BlockSpec(memory_space=pltpu.VMEM)
SMEM = pl.BlockSpec(memory_space=pltpu.SMEM)
LIMIT = 48 * 1024 * 1024


def split(value):
    high = value.astype(jnp.bfloat16)
    return high, (value - high.astype(jnp.float32)).astype(jnp.bfloat16)


def state_kernel(asked_ref, place_ref, speed_ref, radius_ref, cell_ref, state_ref, served_ref):
    alive = jnp.where(cell_ref[...] >= 0, 1.0, 0.0)
    for c in range(3):
        place = place_ref[c]
        state_ref[:, c, :] = (stiffness * place - damping * speed_ref[c]) * alive
        state_ref[:, 4 + c, :] = place
    state_ref[:, 3, :] = alive
    state_ref[:, 7, :] = radius_ref[...] * math.sqrt(2.0 * math.log(2.0))

    def serve(s, _):
        served_ref[s] = state_ref[jnp.clip(asked_ref[s], 0, state_ref.shape[0] - 1)]
        return 0

    lax.fori_loop(0, served_ref.shape[0], serve, 0, unroll=4)


def weights(columns, other):
    one = columns[:, 4:5] - other[4:5, :]
    two = columns[:, 5:6] - other[5:6, :]
    three = columns[:, 6:7] - other[6:7, :]
    reach = columns[:, 7:8] + other[7:8, :]
    dist_sq = one * one + two * two + three * three
    square = reach * reach
    guess = pl.reciprocal(square, approx=True)
    return split(jnp.exp2((dist_sq * guess) * (square * guess - 2.0)))


def stacked(state):
    return jnp.concatenate(split(state), axis=0)


def summed(lhs, pieces, dims):
    high, low = (
        lax.dot_general(lhs, piece, dims, preferred_element_type=jnp.float32) for piece in pieces
    )
    both = high + low
    return both[0:8] + both[8:16]


def contact_kernel(mine_ref, slot_ref, state_ref, partner_ref, acc_ref, back_ref, carry):
    blocks = state_ref.shape[0]
    pairs = mine_ref.shape[0]
    carry[...] = jnp.zeros_like(carry)

    def local(b, _):
        state = state_ref[b]
        after = jnp.minimum(b + 1, blocks - 1)
        beside = state_ref[after] * jnp.where(b + 1 < blocks, 1.0, 0.0)
        both = jnp.concatenate([state, beside], axis=1)
        pieces = weights(state.T, both)
        on_me = summed(stacked(both), pieces, NT)
        on_next = summed(stacked(state), [piece[:, WIDTH:] for piece in pieces], NN)
        acc_ref[b] = on_me + carry[...]
        carry[...] = on_next
        return 0

    lax.fori_loop(0, blocks, local, 0, unroll=4)

    def listed(p, _):
        mine = mine_ref[p]
        slot = slot_ref[p]
        state = state_ref[mine]
        other = partner_ref[slot]
        pieces = weights(state.T, other)
        on_me = summed(stacked(other), pieces, NT)
        on_other = summed(stacked(state), pieces, NN)
        acc_ref[mine] = acc_ref[mine] + on_me
        back_ref[slot] = on_other[0:4]
        return 0

    lax.fori_loop(0, pairs, listed, 0, unroll=4)


def fluid_kernel(tile, owner_ref, cell_ref, speed_ref, radius_ref, table_ref, fluid_ref, deposit_ref, table, total):
    ranks, fields, rows, _ = table_ref.shape
    high, low = split(table_ref[...].reshape(ranks * fields * rows, WIDTH))
    table[:, 0:WIDTH] = high
    table[:, WIDTH:] = low
    total[...] = jnp.zeros_like(total)

    def step(t, _):
        part = pl.ds(pl.multiple_of(t * tile, tile), tile)
        cell = cell_ref[:, part]
        alive = jnp.where(cell >= 0, 1.0, 0.0)
        safe = jnp.maximum(cell, 0)
        brick = safe // (rows * WIDTH)
        owner = jnp.zeros_like(cell)
        for k in range(ranks):
            owner = jnp.where(brick == k, owner_ref[0, k], owner)
        stored = jnp.where(cell >= 0, owner * (rows * WIDTH) + safe % (rows * WIDTH), 0)
        lane = lax.broadcasted_iota(jnp.int32, (WIDTH, tile), 0)
        hot = jnp.where(lane == stored % WIDTH, 1.0, 0.0).astype(jnp.bfloat16)
        row = lax.broadcasted_iota(jnp.int32, (ranks * rows, tile), 0)
        mask = (row == stored // WIDTH).reshape(ranks, 1, rows, tile)
        found = jnp.dot(
            table[...], jnp.concatenate([hot, hot], axis=0), preferred_element_type=jnp.float32
        ).reshape(ranks, fields, rows, tile)
        found = jnp.sum(jnp.where(mask, found, 0.0), axis=(0, 2))
        radii = radius_ref[:, part]
        scale = alive * drag_coeff * radii
        cube = alive * radii * radii * radii
        drags = []
        for c in range(3):
            drag = scale * (found[c : c + 1] - speed_ref[c, :, part])
            fluid_ref[c, :, part] = drag - cube * found[3 + c : 4 + c]
            drags.append(-drag)
        drags = jnp.concatenate(drags, axis=0).reshape(1, 3, 1, tile)
        spread = jnp.where(mask, drags, 0.0).reshape(ranks * 3 * rows, tile)
        high, low = split(spread)
        total[...] += lax.dot_general(
            high, hot, NT, preferred_element_type=jnp.float32
        ) + lax.dot_general(low, hot, NT, preferred_element_type=jnp.float32)
        return 0

    lax.fori_loop(0, cell_ref.shape[1] // tile, step, 0)
    deposit_ref[...] = total[...].reshape(ranks, 3, rows, WIDTH)


def final_kernel(asked_ref, acc_ref, back_ref, state_ref, fluid_ref, speed_ref, radius_ref, out_ref, force):
    force[...] = acc_ref[...]

    def add(s, _):
        block = asked_ref[s]

        @pl.when(block >= 0)
        def _():
            force[block, 0:4, :] = force[block, 0:4, :] + back_ref[s]

        return 0

    lax.fori_loop(0, asked_ref.shape[0], add, 0)
    radii = radius_ref[...]
    scale = time_step / (radii * radii * radii)
    alive = state_ref[:, 3, :]
    weight = force[:, 3, :]
    for c in range(3):
        contact = state_ref[:, c, :] * weight - alive * force[:, c, :]
        out_ref[c] = speed_ref[c] + scale * (contact + fluid_ref[c])


def on_device(
    positions,
    velocities,
    radius,
    sphere_cell,
    pair_route,
    pair_mine,
    pair_theirs,
    brick_owner,
    fluid_velocity,
    pressure_grad,
):
    f32 = jnp.float32
    sphere_total = positions.shape[2]
    blocks = sphere_total // WIDTH
    gy_count = lax.axis_size("gy")
    gx_count = lax.axis_size("gx")
    cells_dev = fluid_velocity.shape[2]
    rows = cells_dev // WIDTH
    pair_total = pair_route.shape[1]
    capacity = max(2, 2 * pair_total // gx_count)
    slot_total = gx_count * capacity
    params = pltpu.CompilerParams(vmem_limit_bytes=LIMIT)

    target = (lax.axis_index("gx") + 1 + pair_route[0, :, 0]) % gx_count
    pair_ids = jnp.arange(pair_total, dtype=jnp.int32)
    earlier = (target[:, None] == target[None, :]) & (pair_ids[None, :] < pair_ids[:, None])
    slot = target * capacity + jnp.sum(earlier.astype(jnp.int32), axis=1)
    match = slot[None, :] == jnp.arange(slot_total, dtype=jnp.int32)[:, None]
    wanted = jnp.sum(jnp.where(match, pair_theirs[0][None, :] + 1, 0), axis=1) - 1
    asked = lax.all_to_all(
        wanted.reshape(gx_count, capacity), "gx", split_axis=0, concat_axis=0, tiled=True
    ).reshape(-1)

    fields = jnp.concatenate([fluid_velocity[:, 0], pressure_grad[:, 0]], axis=0)
    fields = fields.reshape(1, 6, rows, WIDTH)
    table = lax.all_to_all(
        jnp.broadcast_to(fields, (gy_count, 6, rows, WIDTH)),
        "gy",
        split_axis=0,
        concat_axis=0,
        tiled=True,
    )

    states, served = pl.pallas_call(
        state_kernel,
        out_shape=(
            jax.ShapeDtypeStruct((blocks, 8, WIDTH), f32),
            jax.ShapeDtypeStruct((slot_total, 8, WIDTH), f32),
        ),
        in_specs=[SMEM] + [VMEM] * 4,
        out_specs=(VMEM, VMEM),
        compiler_params=params,
        name="states",
    )(
        asked,
        positions.reshape(3, blocks, WIDTH),
        velocities.reshape(3, blocks, WIDTH),
        radius.reshape(blocks, WIDTH),
        sphere_cell.reshape(blocks, WIDTH),
    )
    partner = lax.all_to_all(
        served.reshape(gx_count, capacity, 8, WIDTH), "gx", split_axis=0, concat_axis=0, tiled=True
    ).reshape(slot_total, 8, WIDTH)

    tile = math.gcd(sphere_total, 512)
    fluid, deposit = pl.pallas_call(
        functools.partial(fluid_kernel, tile),
        out_shape=(
            jax.ShapeDtypeStruct((3, 1, sphere_total), f32),
            jax.ShapeDtypeStruct((gy_count, 3, rows, WIDTH), f32),
        ),
        in_specs=[SMEM] + [VMEM] * 4,
        out_specs=(VMEM, VMEM),
        scratch_shapes=[
            pltpu.VMEM((gy_count * 6 * rows, 2 * WIDTH), jnp.bfloat16),
            pltpu.VMEM((gy_count * 3 * rows, WIDTH), f32),
        ],
        compiler_params=params,
        cost_estimate=pl.CostEstimate(flops=4000000000, bytes_accessed=1000000, transcendentals=0),
        name="fluid",
    )(brick_owner, sphere_cell, velocities, radius, table)
    deposits = lax.all_to_all(deposit, "gy", split_axis=0, concat_axis=0, tiled=True)
    drag_source = jnp.sum(deposits, axis=0).reshape(3, 1, cells_dev)

    acc, back = pl.pallas_call(
        contact_kernel,
        out_shape=(
            jax.ShapeDtypeStruct((blocks, 8, WIDTH), f32),
            jax.ShapeDtypeStruct((slot_total, 4, WIDTH), f32),
        ),
        in_specs=[SMEM, SMEM, VMEM, VMEM],
        out_specs=(VMEM, VMEM),
        scratch_shapes=[pltpu.VMEM((8, WIDTH), f32)],
        compiler_params=params,
        cost_estimate=pl.CostEstimate(
            flops=8000000000, bytes_accessed=1500000, transcendentals=6000000
        ),
        name="contact",
    )(pair_mine[0], slot, states, partner)
    returned = lax.all_to_all(
        back.reshape(gx_count, capacity, 4, WIDTH), "gx", split_axis=0, concat_axis=0, tiled=True
    ).reshape(slot_total, 4, WIDTH)
    speed = velocities.reshape(3, blocks, WIDTH)
    new_velocity = pl.pallas_call(
        final_kernel,
        out_shape=jax.ShapeDtypeStruct((3, blocks, WIDTH), f32),
        in_specs=[SMEM] + [VMEM] * 6,
        out_specs=VMEM,
        scratch_shapes=[pltpu.VMEM((blocks, 8, WIDTH), f32)],
        compiler_params=params,
        name="final",
    )(asked, acc, returned, states, fluid.reshape(3, blocks, WIDTH), speed, radius.reshape(blocks, WIDTH))
    return (new_velocity.reshape(3, 1, sphere_total), drag_source)


def solution(mesh):
    placed = (
        P(None, "gx", "gy"),
        P(None, "gx", "gy"),
        P("gx", "gy"),
        P("gx", "gy"),
        P("gx", "gy", None),
        P("gx", "gy"),
        P("gx", "gy"),
        P("gx", None),
        P(None, "gx", "gy"),
        P(None, "gx", "gy"),
    )
    return jax.shard_map(
        on_device,
        mesh=mesh,
        in_specs=placed,
        out_specs=(P(None, "gx", "gy"), P(None, "gx", "gy")),
        check_vma=False,
    )
```

time: 434 us -> 85.5 us (0.20)
  blocking collectives: 169 us -> 0 us
  other arithmetic: 147 us -> 4.3 us
  local copies, waits for them, and re-layouts: 80.6 us -> 2.63 us
  Pallas kernels: 0 us -> 41.4 us
  between operations: 14.4 us -> 0.72 us
  waiting for transfers between devices: 6.04 us -> 14.4 us
  starting transfers between devices: 13 us -> 21.3 us
    all_gather x2 -> x0, blocking collectives: 169 us -> none  [the longest x1 96 us: on_device(): lax.all_gather(pressure_grad, 'gy', axis=2, tiled=True)]
    gather x4 -> x0, local copies, waits for them, and re-layouts: 61.3 us -> none  [the longest x1 29.9 us: on_device(): grad_at = jnp.take(column_p[:, 0], storage, axis=1)]
    scatter-add x1 -> x0, other arithmetic: 54.5 us -> none  [on_device(): jax.ops.segment_sum(-drag_force.T, storage, num_segments=gy_count * cells...]
    reduce_sum x34 -> x3, other arithmetic: 50.7 us -> 0.89 us  [the longest x1 0.62 us: on_device(): drag_source = jnp.sum(deposits, axis=0).reshape(3, 1, cells_dev)]
    pallas_call x0 -> x4, Pallas kernels: none -> 41.4 us  [the longest x1 26.1 us: on_device(): pl.pallas_call(contact_kernel, out_shape=(jax.ShapeDtypeStruct((blocks, 8...]
    sub x32 -> x1, other arithmetic: 14.9 us -> 0.01 us  [on_device(): jnp.sum(jnp.where(match, pair_theirs[0][None, :] + 1, 0), axis=1) - 1]
    mul x35 -> x0, other arithmetic: 12.5 us -> none  [the longest x32 11.5 us: contact(): pulling = weight[:, None] * (stiffness * offset - damping * relative)]
    reshape x1 -> x0, other arithmetic: 10.1 us -> none  [on_device(): return (new_velocity.reshape(3, 1, sphere_total), drag_source)]
  transfers between devices with their start and end apart: 4 -> 5, of which waited for: 1 -> 3; matrix products, arithmetic and copies ran while one was open for 39% -> 3% of each run, Pallas kernels for 0% -> 45%
where the time goes in v1:
time: 85.5 us; the launch traced here: 84.8 us
  Pallas kernels  41.4 us (48%)
  starting transfers between devices  21.3 us (25%)
  waiting for transfers between devices  14.4 us (17%)
  other arithmetic  4.3 us (5%)
  local copies, waits for them, and re-layouts  2.63 us (3%)
    pallas_call x1, Pallas kernels, on_device(): pl.pallas_call(contact_kernel, out_shape=(jax.ShapeDtypeStruct((blocks, 8...  26.1 us
    pallas_call x1, Pallas kernels, on_device(): pl.pallas_call(functools.partial(fluid_kernel, tile), out_shape=(jax.Shap...  10.3 us
    all_to_all x1, waiting for transfers between devices, on_device(): lax.all_to_all(back.reshape(gx_count, capacity, 4, WIDTH), 'gx', split_ax...  6.32 us
    all_to_all x1, starting transfers between devices, on_device(): lax.all_to_all(wanted.reshape(gx_count, capacity), 'gx', split_axis=0, co...  5.17 us
    all_to_all x1, starting transfers between devices, on_device(): lax.all_to_all(jnp.broadcast_to(fields, (gy_count, 6, rows, WIDTH)), 'gy'...  5.01 us
    all_to_all x1, waiting for transfers between devices, on_device(): lax.all_to_all(jnp.broadcast_to(fields, (gy_count, 6, rows, WIDTH)), 'gy'...  4.25 us
    all_to_all x1, starting transfers between devices, on_device(): lax.all_to_all(back.reshape(gx_count, capacity, 4, WIDTH), 'gx', split_ax...  4.19 us
    all_to_all x1, waiting for transfers between devices, on_device(): lax.all_to_all(wanted.reshape(gx_count, capacity), 'gx', split_axis=0, co...  3.83 us
  transfers between devices with their start and end apart: 5, of which 3 were waited for; matrix products, arithmetic and copies ran while one was open for 3% of the time, Pallas kernels for 45%

profile of v1, /device:TPU:0, one launch (start us, length us, event | category | flops | bytes accessed | tf_op | source)
XLA Modules:
  0.0 84.8 jit_solution(16862168980440277115)
XLA Ops:
  0.6 0.0 copy-start.6
  0.6 0.7 and_select_fusion
  1.3 0.2 convert_reduce_fusion
  1.5 0.7 multiply_add_fusion.slot_ref
  2.2 0.7 add_bitcast_fusion
  2.8 0.1 select_reduce_fusion
  2.9 0.7 sub.7
  3.6 5.2 %all-to-all-start = ((s32[8,1,16]{2,1,0:T(1,128)}), s32[8,1,16]{2,1,0:T(1,128)S(1)}, u32[]{:S(2)}, u32[]{:S(2)}) async-start(s32[8,1,16]{2,1,0:T(1,128)} %bitcast.2), calls=%async_computation | async-start | bytes 8192 | tf_op jit(solution)/shard_map/all_to_all | solution.py:198
  8.8 0.0 copy-done.6
  8.8 0.7 maximum_bitcast_fusion
  9.5 3.8 %all-to-all-done = s32[8,1,16]{2,1,0:T(1,128)S(1)} async-done(((s32[8,1,16]{2,1,0:T(1,128)}), s32[8,1,16]{2,1,0:T(1,128)S(1)}, u32[]{:S(2)}, u32[]{:S(2)}) %all-to-all-start) | async-done | bytes 544 | tf_op jit(solution)/shard_map/all_to_all | solution.py:198
  13.4 0.7 broadcast_in_dim.31
  14.1 0.0 copy-start
  14.1 0.0 copy-start.1
  14.1 0.0 copy-start.2
  14.1 0.0 copy-start.3
  14.1 5.0 %all-to-all-start.3 = ((f32[4,6,16,128]{3,2,1,0:T(8,128)}), f32[4,6,16,128]{3,2,1,0:T(8,128)S(1)}, u32[]{:S(2)}, u32[]{:S(2)}) async-start(f32[4,6,16,128]{3,2,1,0:T(8,128)} %broadcast_in_dim.31), calls=%async_computation.3 | async-start | bytes 393216 | tf_op jit(solution)/shard_map/all_to_all | solution.py:204
  19.1 0.5 broadcast.99
  19.6 0.7 reduce.3
  20.3 0.1 reshape.105.asked_ref
  20.3 0.0 copy-done
  20.3 0.0 copy-done.1
  20.3 0.0 copy-done.2
  20.4 0.0 copy-done.3
  20.4 1.9 %states.1 = (f32[64,8,128]{2,1,0:T(8,128)S(1)}, f32[128,8,128]{2,1,0:T(8,128)}) custom-call(s32[128]{0:T(128)S(1)} %reshape.105.asked_ref, f32[3,64,128]{2,1,0:T(8,128)S(1)} %bitcast.29, f32[3,64,128]{2,1,0:T(8,128)S(1)} %bitcast.25, f32[64,128]{1,0:T(8,128)S(1)} %bitcast.27, s32[64,128]{1,0:T(8,128)S(1)} %bitcast.31), custom_call_target="tpu_custom_call" | custom-call | tf_op jit(solution)/shard_map/states/pallas_call | solution.py:212
  22.3 4.3 %all-to-all-done.3.table_ref = f32[4,6,16,128]{3,2,1,0:T(8,128)S(1)} async-done(((f32[4,6,16,128]{3,2,1,0:T(8,128)}), f32[4,6,16,128]{3,2,1,0:T(8,128)S(1)}, u32[]{:S(2)}, u32[]{:S(2)}) %all-to-all-start.3) | async-done | bytes 196640 | tf_op jit(solution)/shard_map/all_to_all | solution.py:204
  26.5 0.0 copy-start.4
  26.5 3.6 %all-to-all-start.1 = ((f32[8,16,8,128]{3,2,1,0:T(8,128)}), f32[8,16,8,128]{3,2,1,0:T(8,128)S(1)}, u32[]{:S(2)}, u32[]{:S(2)}) async-start(f32[8,16,8,128]{3,2,1,0:T(8,128)} %bitcast.8), calls=%async_computation.1 | async-start | bytes 1048576 | tf_op jit(solution)/shard_map/all_to_all | solution.py:229
  30.2 0.0 copy-done.4
  30.2 10.3 %fluid.1 = (f32[3,1,8192]{2,1,0:T(1,128)S(1)}, f32[4,3,16,128]{3,2,1,0:T(8,128)}) custom-call(s32[1,4]{1,0:T(1,128)S(1)} %copy-done.4, s32[1,8192]{1,0:T(1,128)S(1)} %copy-done.3, f32[3,1,8192]{2,1,0:T(1,128)S(1)} %copy-done, f32[1,8192]{1,0:T(1,128)S(1)} %copy-done.1, f32[4,6,16,128]{3,2,1,0:T(8,128)S(1)} %all-to-all-done.3.table_ref), custom_call_target="tpu_custom_call" | custom-call | flops 4000000000 | bytes 1000000 | tf_op jit(solution)/shard_map/fluid/pallas_call | solution.py:234
  40.4 0.0 all-to-all-done.1
  40.4 3.3 %all-to-all-start.4 = ((f32[4,3,16,128]{3,2,1,0:T(8,128)}), f32[4,3,16,128]{3,2,1,0:T(8,128)S(1)}, u32[]{:S(2)}, u32[]{:S(2)}) async-start(f32[4,3,16,128]{3,2,1,0:T(8,128)} %get-tuple-element.13), calls=%async_computation.4 | async-start | bytes 196608 | tf_op jit(solution)/shard_map/all_to_all | solution.py:250
  43.7 0.0 copy-start.5
  43.8 0.6 copy-done.5
  44.4 26.1 %contact.1 = (f32[64,8,128]{2,1,0:T(8,128)S(1)}, f32[128,4,128]{2,1,0:T(4,128)}) custom-call(s32[64]{0:T(128)S(1)} %bitcast.32, s32[64]{0:T(128)S(1)} %multiply_add_fusion.slot_ref, f32[64,8,128]{2,1,0:T(8,128)S(1)} %get-tuple-element.8.state_ref, f32[128,8,128]{2,1,0:T(8,128)S(1)} %bitcast.24), custom_call_target="tpu_custom_call" | custom-call | flops 8000000000 | bytes 1500000 | tf_op jit(solution)/shard_map/contact/pallas_call | solution.py:253
  70.5 0.0 all-to-all-done.4
  70.5 4.2 %all-to-all-start.2 = ((f32[8,16,4,128]{3,2,1,0:T(4,128)}), f32[8,16,4,128]{3,2,1,0:T(4,128)S(1)}, u32[]{:S(2)}, u32[]{:S(2)}) async-start(f32[8,16,4,128]{3,2,1,0:T(4,128)} %bitcast.10), calls=%async_computation.2 | async-start | bytes 524288 | tf_op jit(solution)/shard_map/all_to_all | solution.py:268
  74.7 0.6 reduce_sum.29
  75.4 6.3 %all-to-all-done.2 = f32[8,16,4,128]{3,2,1,0:T(4,128)S(1)} async-done(((f32[8,16,4,128]{3,2,1,0:T(4,128)}), f32[8,16,4,128]{3,2,1,0:T(4,128)S(1)}, u32[]{:S(2)}, u32[]{:S(2)}) %all-to-all-start.2) | async-done | bytes 262176 | tf_op jit(solution)/shard_map/all_to_all | solution.py:268
  81.7 3.1 %final.1 = f32[3,64,128]{2,1,0:T(8,128)} custom-call(s32[128]{0:T(128)S(1)} %reshape.105.asked_ref, f32[64,8,128]{2,1,0:T(8,128)S(1)} %get-tuple-element.10.acc_ref, f32[128,4,128]{2,1,0:T(4,128)S(1)} %bitcast.23, f32[64,8,128]{2,1,0:T(8,128)S(1)} %get-tuple-element.8.state_ref, f32[3,64,128]{2,1,0:T(8,128)S(1)} %bitcast.30, f32[3,64,128]{2,1,0:T(8,128)S(1)} %bitcast.26, ...), custom_call_target="tpu_custom_call" | custom-call | tf_op jit(solution)/shard_map/final/pallas_call | solution.py:272
  (1 shorter events, 0.0 us)
Async XLA Ops:
  0.6 8.2 %copy-start.6 = (f32[3,1,2048]{2,1,0:T(1,128)S(1)}, f32[3,1,2048]{2,1,0:T(1,128)}, u32[]{:S(2)}) copy-start(f32[3,1,2048]{2,1,0:T(1,128)} %param.19) | copy-start | bytes 73732
  3.6 9.8 %all-to-all-start = ((s32[8,1,16]{2,1,0:T(1,128)}), s32[8,1,16]{2,1,0:T(1,128)S(1)}, u32[]{:S(2)}, u32[]{:S(2)}) async-start(s32[8,1,16]{2,1,0:T(1,128)} %bitcast.2), calls=%async_computation | async-start | bytes 8192 | tf_op jit(solution)/shard_map/all_to_all | solution.py:198
  14.1 6.3 %copy-start = (f32[3,1,8192]{2,1,0:T(1,128)S(1)}, f32[3,1,8192]{2,1,0:T(1,128)}, u32[]{:S(2)}) copy-start(f32[3,1,8192]{2,1,0:T(1,128)} %speed_ref.1) | copy-start | bytes 294916
  14.1 6.3 %copy-start.1 = (f32[1,8192]{1,0:T(1,128)S(1)}, f32[1,8192]{1,0:T(1,128)}, u32[]{:S(2)}) copy-start(f32[1,8192]{1,0:T(1,128)} %radius_ref.1) | copy-start | bytes 98308
  14.1 6.3 %copy-start.2 = (f32[3,1,8192]{2,1,0:T(1,128)S(1)}, f32[3,1,8192]{2,1,0:T(1,128)}, u32[]{:S(2)}) copy-start(f32[3,1,8192]{2,1,0:T(1,128)} %param.10) | copy-start | bytes 294916
  14.1 6.3 %copy-start.3 = (s32[1,8192]{1,0:T(1,128)S(1)}, s32[1,8192]{1,0:T(1,128)}, u32[]{:S(2)}) copy-start(s32[1,8192]{1,0:T(1,128)} %cell_ref.1) | copy-start | bytes 98308
  14.1 12.5 %all-to-all-start.3 = ((f32[4,6,16,128]{3,2,1,0:T(8,128)}), f32[4,6,16,128]{3,2,1,0:T(8,128)S(1)}, u32[]{:S(2)}, u32[]{:S(2)}) async-start(f32[4,6,16,128]{3,2,1,0:T(8,128)} %broadcast_in_dim.31), calls=%async_computation.3 | async-start | bytes 393216 | tf_op jit(solution)/shard_map/all_to_all | solution.py:204
  26.5 3.6 %copy-start.4 = (s32[1,4]{1,0:T(1,128)S(1)}, s32[1,4]{1,0:T(1,128)}, u32[]{:S(2)}) copy-start(s32[1,4]{1,0:T(1,128)} %owner_ref.1) | copy-start | bytes 52
  26.5 13.9 %all-to-all-start.1 = ((f32[8,16,8,128]{3,2,1,0:T(8,128)}), f32[8,16,8,128]{3,2,1,0:T(8,128)S(1)}, u32[]{:S(2)}, u32[]{:S(2)}) async-start(f32[8,16,8,128]{3,2,1,0:T(8,128)} %bitcast.8), calls=%async_computation.1 | async-start | bytes 1048576 | tf_op jit(solution)/shard_map/all_to_all | solution.py:229
  40.4 30.1 %all-to-all-start.4 = ((f32[4,3,16,128]{3,2,1,0:T(8,128)}), f32[4,3,16,128]{3,2,1,0:T(8,128)S(1)}, u32[]{:S(2)}, u32[]{:S(2)}) async-start(f32[4,3,16,128]{3,2,1,0:T(8,128)} %get-tuple-element.13), calls=%async_computation.4 | async-start | bytes 196608 | tf_op jit(solution)/shard_map/all_to_all | solution.py:250
  43.7 0.7 copy-start.5
  70.5 11.1 %all-to-all-start.2 = ((f32[8,16,4,128]{3,2,1,0:T(4,128)}), f32[8,16,4,128]{3,2,1,0:T(4,128)S(1)}, u32[]{:S(2)}, u32[]{:S(2)}) async-start(f32[8,16,4,128]{3,2,1,0:T(4,128)} %bitcast.10), calls=%async_computation.2 | async-start | bytes 524288 | tf_op jit(solution)/shard_map/all_to_all | solution.py:268

commit v2 on v1

--- a/solution.py
+++ b/solution.py
@@ -25,6 +25,71 @@
     return high, (value - high.astype(jnp.float32)).astype(jnp.bfloat16)
 
 
+def greet(counts):
+    barrier = pltpu.get_barrier_semaphore()
+    total = 0
+    for axis, count in counts.items():
+        me = lax.axis_index(axis)
+        for step in range(1, count):
+            pl.semaphore_signal(
+                barrier,
+                inc=1,
+                device_id={axis: lax.rem(me + step, count)},
+                device_id_type=pl.DeviceIdType.MESH,
+            )
+        total += count - 1
+    pl.semaphore_wait(barrier, total)
+
+
+def start_copies(axis, count, source, landing, send_sem, recv_sem, same=False):
+    me = lax.axis_index(axis)
+    copies = []
+    for step in range(1, count):
+        peer = lax.rem(me + step, count)
+        copy = pltpu.make_async_remote_copy(
+            src_ref=source if same else source.at[peer],
+            dst_ref=landing.at[me],
+            send_sem=send_sem.at[step],
+            recv_sem=recv_sem.at[step],
+            device_id={axis: peer},
+            device_id_type=pl.DeviceIdType.MESH,
+        )
+        copy.start()
+        copies.append(copy)
+    return copies
+
+
+def exchange_kernel(counts, gx_ref, gy_ref, gx_out, gy_out, xs, xr, ys, yr):
+    greet(counts)
+    copies = start_copies("gx", counts["gx"], gx_ref, gx_out, xs, xr)
+    copies += start_copies("gy", counts["gy"], gy_ref, gy_out, ys, yr, True)
+    me = lax.axis_index("gx")
+    gx_out[me] = gx_ref[me]
+    me = lax.axis_index("gy")
+    gy_out[me] = gy_ref[...]
+    for copy in copies:
+        copy.wait()
+
+
+def exchange(counts, gx_value, gy_value):
+    return pl.pallas_call(
+        functools.partial(exchange_kernel, counts),
+        out_shape=(
+            jax.ShapeDtypeStruct(gx_value.shape, gx_value.dtype),
+            jax.ShapeDtypeStruct((counts["gy"],) + gy_value.shape, gy_value.dtype),
+        ),
+        in_specs=[VMEM, VMEM],
+        out_specs=(VMEM, VMEM),
+        scratch_shapes=[
+            pltpu.SemaphoreType.DMA((counts[axis],)) for axis in ("gx", "gx", "gy", "gy")
+        ],
+        compiler_params=pltpu.CompilerParams(
+            vmem_limit_bytes=LIMIT, collective_id=0, has_side_effects=True
+        ),
+        name="exchange",
+    )(gx_value, gy_value)
+
+
 def state_kernel(asked_ref, place_ref, speed_ref, radius_ref, cell_ref, state_ref, served_ref):
     alive = jnp.where(cell_ref[...] >= 0, 1.0, 0.0)
     for c in range(3):
@@ -64,24 +129,8 @@
     return both[0:8] + both[8:16]
 
 
-def contact_kernel(mine_ref, slot_ref, state_ref, partner_ref, acc_ref, back_ref, carry):
-    blocks = state_ref.shape[0]
-    pairs = mine_ref.shape[0]
-    carry[...] = jnp.zeros_like(carry)
-
-    def local(b, _):
-        state = state_ref[b]
-        after = jnp.minimum(b + 1, blocks - 1)
-        beside = state_ref[after] * jnp.where(b + 1 < blocks, 1.0, 0.0)
-        both = jnp.concatenate([state, beside], axis=1)
-        pieces = weights(state.T, both)
-        on_me = summed(stacked(both), pieces, NT)
-        on_next = summed(stacked(state), [piece[:, WIDTH:] for piece in pieces], NN)
-        acc_ref[b] = on_me + carry[...]
-        carry[...] = on_next
-        return 0
-
-    lax.fori_loop(0, blocks, local, 0, unroll=4)
+def listed_kernel(mine_ref, slot_ref, state_ref, partner_ref, acc_ref, back_ref):
+    acc_ref[...] = jnp.zeros_like(acc_ref)
 
     def listed(p, _):
         mine = mine_ref[p]
@@ -92,13 +141,63 @@
         on_me = summed(stacked(other), pieces, NT)
         on_other = summed(stacked(state), pieces, NN)
         acc_ref[mine] = acc_ref[mine] + on_me
-        back_ref[slot] = on_other[0:4]
+        back_ref[pl.ds(pl.multiple_of(slot * 4, 4), 4), :] = on_other[0:4]
         return 0
 
-    lax.fori_loop(0, pairs, listed, 0, unroll=4)
-
-
-def fluid_kernel(tile, owner_ref, cell_ref, speed_ref, radius_ref, table_ref, fluid_ref, deposit_ref, table, total):
+    lax.fori_loop(0, mine_ref.shape[0], listed, 0, unroll=4)
+
+
+def local_kernel(
+    counts, state_ref, listed_ref, gx_ref, gy_ref, acc_ref, gx_out, gy_out, carry, xs, xr, ys, yr
+):
+    greet(counts)
+    copies = start_copies("gx", counts["gx"], gx_ref, gx_out, xs, xr)
+    copies += start_copies("gy", counts["gy"], gy_ref, gy_out, ys, yr)
+    me = lax.axis_index("gx")
+    gx_out[me] = gx_ref[me]
+    me = lax.axis_index("gy")
+    gy_out[me] = gy_ref[me]
+    blocks = state_ref.shape[0]
+    carry[...] = jnp.zeros_like(carry)
+
+    def local(b, _):
+        state = state_ref[b]
+        after = lax.rem(b + 1, blocks)
+        beside = state_ref[after] * jnp.where(after > 0, 1.0, 0.0)
+        both = jnp.concatenate([state, beside], axis=1)
+        pieces = weights(state.T, both)
+        on_me = summed(stacked(both), pieces, NT)
+        on_next = summed(stacked(state), [piece[:, WIDTH:] for piece in pieces], NN)
+        acc_ref[b] = listed_ref[b] + on_me + carry[...]
+        carry[...] = on_next
+        return 0
+
+    lax.fori_loop(0, blocks, local, 0, unroll=4)
+    for copy in copies:
+        copy.wait()
+
+
+def fluid_kernel(
+    tile,
+    gx_count,
+    owner_ref,
+    cell_ref,
+    speed_ref,
+    radius_ref,
+    table_ref,
+    served_ref,
+    fluid_ref,
+    deposit_ref,
+    partner_ref,
+    table,
+    total,
+    send_sem,
+    recv_sem,
+):
+    greet({"gx": gx_count})
+    copies = start_copies("gx", gx_count, served_ref, partner_ref, send_sem, recv_sem)
+    me = lax.axis_index("gx")
+    partner_ref[me] = served_ref[me]
     ranks, fields, rows, _ = table_ref.shape
     high, low = split(table_ref[...].reshape(ranks * fields * rows, WIDTH))
     table[:, 0:WIDTH] = high
@@ -141,9 +240,24 @@
 
     lax.fori_loop(0, cell_ref.shape[1] // tile, step, 0)
     deposit_ref[...] = total[...].reshape(ranks, 3, rows, WIDTH)
-
-
-def final_kernel(asked_ref, acc_ref, back_ref, state_ref, fluid_ref, speed_ref, radius_ref, out_ref, force):
+    for copy in copies:
+        copy.wait()
+
+
+def final_kernel(
+    asked_ref,
+    acc_ref,
+    back_ref,
+    state_ref,
+    fluid_ref,
+    speed_ref,
+    radius_ref,
+    deposits_ref,
+    out_ref,
+    source_ref,
+    force,
+):
+    source_ref[...] = jnp.sum(deposits_ref[...], axis=0)
     force[...] = acc_ref[...]
 
     def add(s, _):
@@ -151,7 +265,7 @@
 
         @pl.when(block >= 0)
         def _():
-            force[block, 0:4, :] = force[block, 0:4, :] + back_ref[s]
+            force[block, 0:4, :] = force[block, 0:4, :] + back_ref[pl.ds(pl.multiple_of(s * 4, 4), 4), :]
 
         return 0
 
@@ -189,25 +303,22 @@
     slot_total = gx_count * capacity
     params = pltpu.CompilerParams(vmem_limit_bytes=LIMIT)
 
+    counts = {"gx": gx_count, "gy": gy_count}
+
     target = (lax.axis_index("gx") + 1 + pair_route[0, :, 0]) % gx_count
     pair_ids = jnp.arange(pair_total, dtype=jnp.int32)
     earlier = (target[:, None] == target[None, :]) & (pair_ids[None, :] < pair_ids[:, None])
     slot = target * capacity + jnp.sum(earlier.astype(jnp.int32), axis=1)
     match = slot[None, :] == jnp.arange(slot_total, dtype=jnp.int32)[:, None]
     wanted = jnp.sum(jnp.where(match, pair_theirs[0][None, :] + 1, 0), axis=1) - 1
-    asked = lax.all_to_all(
-        wanted.reshape(gx_count, capacity), "gx", split_axis=0, concat_axis=0, tiled=True
-    ).reshape(-1)
-
+    wanted = jnp.pad(
+        wanted.reshape(gx_count, 1, capacity),
+        ((0, 0), (0, 0), (0, WIDTH - capacity)),
+        constant_values=-1,
+    )
     fields = jnp.concatenate([fluid_velocity[:, 0], pressure_grad[:, 0]], axis=0)
-    fields = fields.reshape(1, 6, rows, WIDTH)
-    table = lax.all_to_all(
-        jnp.broadcast_to(fields, (gy_count, 6, rows, WIDTH)),
-        "gy",
-        split_axis=0,
-        concat_axis=0,
-        tiled=True,
-    )
+    asked, table = exchange(counts, wanted, fields.reshape(6, rows, WIDTH))
+    asked = asked[:, 0, :capacity].reshape(-1)
 
     states, served = pl.pallas_call(
         state_kernel,
@@ -226,59 +337,87 @@
         radius.reshape(blocks, WIDTH),
         sphere_cell.reshape(blocks, WIDTH),
     )
-    partner = lax.all_to_all(
-        served.reshape(gx_count, capacity, 8, WIDTH), "gx", split_axis=0, concat_axis=0, tiled=True
-    ).reshape(slot_total, 8, WIDTH)
-
     tile = math.gcd(sphere_total, 512)
-    fluid, deposit = pl.pallas_call(
-        functools.partial(fluid_kernel, tile),
+    fluid, deposit, partner = pl.pallas_call(
+        functools.partial(fluid_kernel, tile, gx_count),
         out_shape=(
             jax.ShapeDtypeStruct((3, 1, sphere_total), f32),
             jax.ShapeDtypeStruct((gy_count, 3, rows, WIDTH), f32),
-        ),
-        in_specs=[SMEM] + [VMEM] * 4,
-        out_specs=(VMEM, VMEM),
+            jax.ShapeDtypeStruct((gx_count, capacity * 8, WIDTH), f32),
+        ),
+        in_specs=[SMEM] + [VMEM] * 5,
+        out_specs=(VMEM, VMEM, VMEM),
         scratch_shapes=[
             pltpu.VMEM((gy_count * 6 * rows, 2 * WIDTH), jnp.bfloat16),
             pltpu.VMEM((gy_count * 3 * rows, WIDTH), f32),
+            pltpu.SemaphoreType.DMA((gx_count,)),
+            pltpu.SemaphoreType.DMA((gx_count,)),
         ],
-        compiler_params=params,
+        compiler_params=pltpu.CompilerParams(
+            vmem_limit_bytes=LIMIT, collective_id=1, has_side_effects=True
+        ),
         cost_estimate=pl.CostEstimate(flops=4000000000, bytes_accessed=1000000, transcendentals=0),
         name="fluid",
-    )(brick_owner, sphere_cell, velocities, radius, table)
-    deposits = lax.all_to_all(deposit, "gy", split_axis=0, concat_axis=0, tiled=True)
-    drag_source = jnp.sum(deposits, axis=0).reshape(3, 1, cells_dev)
-
-    acc, back = pl.pallas_call(
-        contact_kernel,
+    )(
+        brick_owner,
+        sphere_cell,
+        velocities,
+        radius,
+        table,
+        served.reshape(gx_count, capacity * 8, WIDTH),
+    )
+    partner = partner.reshape(slot_total, 8, WIDTH)
+    listed, back = pl.pallas_call(
+        listed_kernel,
         out_shape=(
             jax.ShapeDtypeStruct((blocks, 8, WIDTH), f32),
-            jax.ShapeDtypeStruct((slot_total, 4, WIDTH), f32),
+            jax.ShapeDtypeStruct((slot_total * 4, WIDTH), f32),
         ),
         in_specs=[SMEM, SMEM, VMEM, VMEM],
         out_specs=(VMEM, VMEM),
-        scratch_shapes=[pltpu.VMEM((8, WIDTH), f32)],
         compiler_params=params,
-        cost_estimate=pl.CostEstimate(
-            flops=8000000000, bytes_accessed=1500000, transcendentals=6000000
-        ),
-        name="contact",
+        name="listed",
     )(pair_mine[0], slot, states, partner)
-    returned = lax.all_to_all(
-        back.reshape(gx_count, capacity, 4, WIDTH), "gx", split_axis=0, concat_axis=0, tiled=True
-    ).reshape(slot_total, 4, WIDTH)
+    acc, returned, deposits = pl.pallas_call(
+        functools.partial(local_kernel, counts),
+        out_shape=(
+            jax.ShapeDtypeStruct((blocks, 8, WIDTH), f32),
+            jax.ShapeDtypeStruct((gx_count, capacity * 4, WIDTH), f32),
+            jax.ShapeDtypeStruct(deposit.shape, f32),
+        ),
+        in_specs=[VMEM] * 4,
+        out_specs=(VMEM, VMEM, VMEM),
+        scratch_shapes=[pltpu.VMEM((8, WIDTH), f32)]
+        + [pltpu.SemaphoreType.DMA((counts[axis],)) for axis in ("gx", "gx", "gy", "gy")],
+        compiler_params=pltpu.CompilerParams(
+            vmem_limit_bytes=LIMIT, collective_id=2, has_side_effects=True
+        ),
+        name="local",
+    )(states, listed, back.reshape(gx_count, capacity * 4, WIDTH), deposit)
+    returned = returned.reshape(slot_total * 4, WIDTH)
     speed = velocities.reshape(3, blocks, WIDTH)
-    new_velocity = pl.pallas_call(
+    new_velocity, drag_source = pl.pallas_call(
         final_kernel,
-        out_shape=jax.ShapeDtypeStruct((3, blocks, WIDTH), f32),
-        in_specs=[SMEM] + [VMEM] * 6,
-        out_specs=VMEM,
+        out_shape=(
+            jax.ShapeDtypeStruct((3, blocks, WIDTH), f32),
+            jax.ShapeDtypeStruct((3, rows, WIDTH), f32),
+        ),
+        in_specs=[SMEM] + [VMEM] * 7,
+        out_specs=(VMEM, VMEM),
         scratch_shapes=[pltpu.VMEM((blocks, 8, WIDTH), f32)],
         compiler_params=params,
         name="final",
-    )(asked, acc, returned, states, fluid.reshape(3, blocks, WIDTH), speed, radius.reshape(blocks, WIDTH))
-    return (new_velocity.reshape(3, 1, sphere_total), drag_source)
+    )(
+        asked,
+        acc,
+        returned,
+        states,
+        fluid.reshape(3, blocks, WIDTH),
+        speed,
+        radius.reshape(blocks, WIDTH),
+        deposits,
+    )
+    return (new_velocity.reshape(3, 1, sphere_total), drag_source.reshape(3, 1, cells_dev))
 
 
 def solution(mesh):

time: 85.5 us -> 61.1 us (0.71)
  starting transfers between devices: 21.3 us -> 0 us
  waiting for transfers between devices: 14.4 us -> 0 us
  Pallas kernels: 41.4 us -> 55.3 us
  other arithmetic: 4.3 us -> 2.4 us
    all_to_all x5 -> x0, starting transfers between devices: 21.3 us -> none  [the longest x1 5.17 us: on_device(): lax.all_to_all(wanted.reshape(gx_count, capacity), 'gx', split_axis=0, co...]
    pallas_call x3 -> x5, Pallas kernels: 39.5 us -> 54.2 us  [the longest x1 16.1 us: on_device(): pl.pallas_call(functools.partial(local_kernel, counts), out_shape=(jax.Sh...]
    all_to_all x5 -> x0, waiting for transfers between devices: 14.4 us -> none  [the longest x1 6.32 us: on_device(): lax.all_to_all(back.reshape(gx_count, capacity, 4, WIDTH), 'gx', split_ax...]
    unnamed x14 -> x16, local copies, waits for them, and re-layouts: 0.67 us -> 2.21 us
  transfers between devices with their start and end apart: 5 -> 0, of which waited for: 3 -> 0; matrix products, arithmetic and copies ran while one was open for 3% -> 0% of each run, Pallas kernels for 45% -> 0%
where the time goes in v2:
time: 61.1 us; the launch traced here: 60.9 us
  Pallas kernels  55.3 us (91%)
  other arithmetic  2.4 us (4%)
  local copies, waits for them, and re-layouts  2.39 us (4%)
  between operations  0.77 us (1%)
    pallas_call x1, Pallas kernels, on_device(): pl.pallas_call(functools.partial(local_kernel, counts), out_shape=(jax.Sh...  16.1 us
    pallas_call x1, Pallas kernels, on_device(): pl.pallas_call(listed_kernel, out_shape=(jax.ShapeDtypeStruct((blocks, 8,...  12.6 us
    pallas_call x1, Pallas kernels, exchange(): pl.pallas_call(functools.partial(exchange_kernel, counts), out_shape=(jax...  11.3 us
    pallas_call x1, Pallas kernels, on_device(): pl.pallas_call(functools.partial(fluid_kernel, tile, gx_count), out_shape...  11 us
    pallas_call x1, Pallas kernels, on_device(): pl.pallas_call(final_kernel, out_shape=(jax.ShapeDtypeStruct((3, blocks,...  3.15 us
    unnamed x16, local copies, waits for them, and re-layouts  2.21 us

profile of v2, /device:TPU:0, one launch (start us, length us, event | category | flops | bytes accessed | tf_op | source)
XLA Modules:
  0.0 60.9 jit_solution(6570923106686149613)
XLA Ops:
  0.6 0.0 copy-start.6
  0.6 0.0 copy-start.7
  0.7 0.0 copy-start
  0.7 0.7 %add_bitcast_fusion = s32[64]{0:T(128)S(1)} fusion(s32[1,64]{1,0:T(1,128)} %param.16), kind=kLoop, calls=%fused_computation.11 | loop fusion | flops 64 | bytes 512 | tf_op jit(solution)/shard_map/jit(_where)/broadcast_in_dim | solution.py:313
  1.4 0.7 %and_select_fusion = s32[64]{0:T(128)S(1)} fusion(s32[1,64,1]{1,2,0:T(1,128)} %param.14, s32[]{:T(128)S(6)} %add.60), kind=kLoop, calls=%fused_computation.9 | loop fusion | flops 768 | bytes 516 | tf_op jit(solution)/shard_map/jit(remainder)/select_n | solution.py:308
  2.0 0.2 convert_reduce_fusion
  2.2 0.0 copy-done.7
  2.2 0.1 select_reduce_fusion
  2.3 0.1 sub.7
  2.4 0.0 copy-done.6
  2.4 0.7 %pad_maximum_fusion.gy_ref = f32[6,16,128]{2,1,0:T(8,128)S(1)} fusion(f32[3,16,128]{2,1,0:T(8,128)S(1)} %bitcast.33, f32[3,16,128]{2,1,0:T(8,128)} %bitcast.34), kind=kLoop, calls=%fused_computation | loop fusion | flops 12288 | bytes 98304 | tf_op jit(solution)/shard_map/concatenate | solution.py:319
  3.2 0.0 copy-start.1
  3.2 0.0 copy-start.3
  3.2 11.3 %exchange.1 = (s32[8,1,128]{2,1,0:T(1,128)S(1)}, f32[4,6,16,128]{3,2,1,0:T(8,128)S(1)}) custom-call(s32[8,1,128]{2,1,0:T(1,128)S(1)} %pad.4.gx_ref, f32[6,16,128]{2,1,0:T(8,128)S(1)} %pad_maximum_fusion.gy_ref), custom_call_target="tpu_custom_call" | custom-call | tf_op jit(solution)/shard_map/exchange/pallas_call | solution.py:75
  14.6 0.1 reshape_squeeze.3.asked_ref
  14.6 0.0 copy-done
  14.6 0.0 copy-done.1
  14.6 0.0 copy-done.3
  14.7 0.0 copy-start.2
  14.7 0.9 %copy-done.2 = f32[3,1,8192]{2,1,0:T(1,128)S(1)} copy-done((f32[3,1,8192]{2,1,0:T(1,128)S(1)}, f32[3,1,8192]{2,1,0:T(1,128)}, u32[]{:S(2)}) %copy-start.2) | copy-done | bytes 98328
  15.6 1.1 %states.1 = (f32[64,8,128]{2,1,0:T(8,128)S(1)}, f32[128,8,128]{2,1,0:T(8,128)S(1)}) custom-call(s32[128]{0:T(128)S(1)} %reshape_squeeze.3.asked_ref, f32[3,64,128]{2,1,0:T(8,128)S(1)} %bitcast.28, f32[3,64,128]{2,1,0:T(8,128)S(1)} %bitcast.22, f32[64,128]{1,0:T(8,128)S(1)} %bitcast.26, s32[64,128]{1,0:T(8,128)S(1)} %bitcast.30), custom_call_target="tpu_custom_call" | custom-call | tf_op jit(solution)/shard_map/states/pallas_call | solution.py:323
  16.7 0.0 copy-start.5
  16.7 0.6 %copy-done.5 = s32[1,4]{1,0:T(1,128)S(1)} copy-done((s32[1,4]{1,0:T(1,128)S(1)}, s32[1,4]{1,0:T(1,128)}, u32[]{:S(2)}) %copy-start.5) | copy-done | bytes 40
  17.3 11.0 %fluid.1 = (f32[3,1,8192]{2,1,0:T(1,128)S(1)}, f32[4,3,16,128]{3,2,1,0:T(8,128)S(1)}, f32[8,128,128]{2,1,0:T(8,128)S(1)}) custom-call(s32[1,4]{1,0:T(1,128)S(1)} %copy-done.5, s32[1,8192]{1,0:T(1,128)S(1)} %copy-done.3, f32[3,1,8192]{2,1,0:T(1,128)S(1)} %copy-done, f32[1,8192]{1,0:T(1,128)S(1)} %copy-done.1, ...), custom_call_target="tpu_custom_call" | custom-call | flops 4000000000 | bytes 1000000 | tf_op jit(solution)/shard_map/fluid/pallas_call | solution.py:341
  28.3 0.0 copy-start.4
  28.3 0.6 %copy-done.4 = s32[1,64]{1,0:T(1,128)S(1)} copy-done((s32[1,64]{1,0:T(1,128)S(1)}, s32[1,64]{1,0:T(1,128)}, u32[]{:S(2)}) %copy-start.4) | copy-done | bytes 280
  29.0 12.6 %listed.1 = (f32[64,8,128]{2,1,0:T(8,128)S(1)}, f32[512,128]{1,0:T(8,128)S(1)}) custom-call(s32[64]{0:T(128)S(1)} %bitcast.31, s32[64]{0:T(128)S(1)} %multiply_add_fusion.slot_ref, f32[64,8,128]{2,1,0:T(8,128)S(1)} %get-tuple-element.17.state_ref, f32[128,8,128]{2,1,0:T(8,128)S(1)} %bitcast.21), custom_call_target="tpu_custom_call" | custom-call | tf_op jit(solution)/shard_map/listed/pallas_call | solution.py:370
  41.6 16.1 %local.1 = (f32[64,8,128]{2,1,0:T(8,128)S(1)}, f32[8,64,128]{2,1,0:T(8,128)S(1)}, f32[4,3,16,128]{3,2,1,0:T(8,128)S(1)}) custom-call(f32[64,8,128]{2,1,0:T(8,128)S(1)} %get-tuple-element.17.state_ref, f32[64,8,128]{2,1,0:T(8,128)S(1)} %get-tuple-element.21.listed_ref, f32[8,64,128]{2,1,0:T(8,128)S(1)} %bitcast.24, f32[4,3,16,128]{3,2,1,0:T(8,128)S(1)} %get-tuple-element.23.gy_ref), custom_call_target="tpu_custom_call" | custom-call | tf_op jit(solution)/shard_map/local/pallas_call | solution.py:381
  57.7 3.1 %final.1 = (f32[3,64,128]{2,1,0:T(8,128)}, f32[3,16,128]{2,1,0:T(8,128)}) custom-call(s32[128]{0:T(128)S(1)} %reshape_squeeze.3.asked_ref, f32[64,8,128]{2,1,0:T(8,128)S(1)} %get-tuple-element.24.acc_ref, f32[512,128]{1,0:T(8,128)S(1)} %bitcast.25, f32[64,8,128]{2,1,0:T(8,128)S(1)} %get-tuple-element.17.state_ref, f32[3,64,128]{2,1,0:T(8,128)S(1)} %bitcast.29, ...), custom_call_target="tpu_custom_call" | custom-call | tf_op jit(solution)/shard_map/final/pallas_call | solution.py:399
  (4 shorter events, 0.0 us)
Async XLA Ops:
  0.6 1.8 %copy-start.6 = (f32[3,1,2048]{2,1,0:T(1,128)S(1)}, f32[3,1,2048]{2,1,0:T(1,128)}, u32[]{:S(2)}) copy-start(f32[3,1,2048]{2,1,0:T(1,128)} %param.19) | copy-start | bytes 73732
  0.6 1.6 %copy-start.7 = (s32[1,64,1]{1,2,0:T(1,128)S(1)}, s32[1,64,1]{1,2,0:T(1,128)}, u32[]{:S(2)}) copy-start(s32[1,64,1]{1,2,0:T(1,128)} %param.14) | copy-start | bytes 772
  0.7 14.0 %copy-start = (f32[3,1,8192]{2,1,0:T(1,128)S(1)}, f32[3,1,8192]{2,1,0:T(1,128)}, u32[]{:S(2)}) copy-start(f32[3,1,8192]{2,1,0:T(1,128)} %speed_ref.1) | copy-start | bytes 294916
  3.2 11.5 %copy-start.1 = (f32[1,8192]{1,0:T(1,128)S(1)}, f32[1,8192]{1,0:T(1,128)}, u32[]{:S(2)}) copy-start(f32[1,8192]{1,0:T(1,128)} %radius_ref.1) | copy-start | bytes 98308
  3.2 11.5 %copy-start.3 = (s32[1,8192]{1,0:T(1,128)S(1)}, s32[1,8192]{1,0:T(1,128)}, u32[]{:S(2)}) copy-start(s32[1,8192]{1,0:T(1,128)} %cell_ref.1) | copy-start | bytes 98308
  14.7 0.9 %copy-start.2 = (f32[3,1,8192]{2,1,0:T(1,128)S(1)}, f32[3,1,8192]{2,1,0:T(1,128)}, u32[]{:S(2)}) copy-start(f32[3,1,8192]{2,1,0:T(1,128)} %param.10) | copy-start | bytes 294916
  16.7 0.7 %copy-start.5 = (s32[1,4]{1,0:T(1,128)S(1)}, s32[1,4]{1,0:T(1,128)}, u32[]{:S(2)}) copy-start(s32[1,4]{1,0:T(1,128)} %owner_ref.1) | copy-start | bytes 52
  28.3 0.7 %copy-start.4 = (s32[1,64]{1,0:T(1,128)S(1)}, s32[1,64]{1,0:T(1,128)}, u32[]{:S(2)}) copy-start(s32[1,64]{1,0:T(1,128)} %param.15) | copy-start | bytes 772

commit v3 on v2

--- a/solution.py
+++ b/solution.py
@@ -132,19 +132,28 @@
 def listed_kernel(mine_ref, slot_ref, state_ref, partner_ref, acc_ref, back_ref):
     acc_ref[...] = jnp.zeros_like(acc_ref)
 
-    def listed(p, _):
-        mine = mine_ref[p]
-        slot = slot_ref[p]
-        state = state_ref[mine]
-        other = partner_ref[slot]
-        pieces = weights(state.T, other)
-        on_me = summed(stacked(other), pieces, NT)
-        on_other = summed(stacked(state), pieces, NN)
-        acc_ref[mine] = acc_ref[mine] + on_me
-        back_ref[pl.ds(pl.multiple_of(slot * 4, 4), 4), :] = on_other[0:4]
+    pairs = mine_ref.shape[0]
+    batch = math.gcd(pairs, 8)
+
+    def listed(step, _):
+        found = []
+        states = [state_ref[mine_ref[step * batch + k]] for k in range(batch)]
+        columns = jnp.concatenate(states, axis=0).T
+        for k in range(batch):
+            mine = mine_ref[step * batch + k]
+            slot = slot_ref[step * batch + k]
+            state = states[k]
+            other = partner_ref[slot]
+            pieces = weights(columns[:, 8 * k : 8 * k + 8], other)
+            on_me = summed(stacked(other), pieces, NT)
+            on_other = summed(stacked(state), pieces, NN)
+            found.append((mine, slot, on_me, on_other))
+        for mine, slot, on_me, on_other in found:
+            acc_ref[mine] = acc_ref[mine] + on_me
+            back_ref[pl.ds(pl.multiple_of(slot * 4, 4), 4), :] = on_other[0:4]
         return 0
 
-    lax.fori_loop(0, mine_ref.shape[0], listed, 0, unroll=4)
+    lax.fori_loop(0, pairs // batch, listed, 0)
 
 
 def local_kernel(
@@ -160,19 +169,29 @@
     blocks = state_ref.shape[0]
     carry[...] = jnp.zeros_like(carry)
 
-    def local(b, _):
-        state = state_ref[b]
-        after = lax.rem(b + 1, blocks)
-        beside = state_ref[after] * jnp.where(after > 0, 1.0, 0.0)
-        both = jnp.concatenate([state, beside], axis=1)
-        pieces = weights(state.T, both)
-        on_me = summed(stacked(both), pieces, NT)
-        on_next = summed(stacked(state), [piece[:, WIDTH:] for piece in pieces], NN)
-        acc_ref[b] = listed_ref[b] + on_me + carry[...]
-        carry[...] = on_next
+    batch = math.gcd(blocks, 8)
+
+    def local(step, _):
+        first = step * batch
+        states = [state_ref[first + k] for k in range(batch)]
+        after = lax.rem(first + batch, blocks)
+        columns = jnp.concatenate(states, axis=0).T
+        states.append(state_ref[after] * jnp.where(after > 0, 1.0, 0.0))
+        found = []
+        for k in range(batch):
+            both = jnp.concatenate(states[k : k + 2], axis=1)
+            pieces = weights(columns[:, 8 * k : 8 * k + 8], both)
+            on_me = summed(stacked(both), pieces, NT)
+            on_next = summed(stacked(states[k]), [piece[:, WIDTH:] for piece in pieces], NN)
+            found.append((on_me, on_next))
+        before = carry[...]
+        for k in range(batch):
+            acc_ref[first + k] = listed_ref[first + k] + found[k][0] + before
+            before = found[k][1]
+        carry[...] = before
         return 0
 
-    lax.fori_loop(0, blocks, local, 0, unroll=4)
+    lax.fori_loop(0, blocks // batch, local, 0)
     for copy in copies:
         copy.wait()
 
@@ -337,7 +356,7 @@
         radius.reshape(blocks, WIDTH),
         sphere_cell.reshape(blocks, WIDTH),
     )
-    tile = math.gcd(sphere_total, 512)
+    tile = math.gcd(sphere_total, 1024)
     fluid, deposit, partner = pl.pallas_call(
         functools.partial(fluid_kernel, tile, gx_count),
         out_shape=(

time: 61.1 us -> 50.5 us (0.83)
  Pallas kernels: 55.3 us -> 44.6 us
    pallas_call x1, Pallas kernels: 16.1 us -> 11.7 us  [on_device(): pl.pallas_call(functools.partial(local_kernel, counts), out_shape=(jax.Sh...]
    pallas_call x1, Pallas kernels: 12.6 us -> 8.73 us  [on_device(): pl.pallas_call(listed_kernel, out_shape=(jax.ShapeDtypeStruct((blocks, 8,...]
    pallas_call x1, Pallas kernels: 11 us -> 8.58 us  [on_device(): pl.pallas_call(functools.partial(fluid_kernel, tile, gx_count), out_shape...]
where the time goes in v3:
time: 50.5 us; the launch traced here: 50.2 us
  Pallas kernels  44.6 us (88%)
  other arithmetic  2.4 us (5%)
  local copies, waits for them, and re-layouts  2.39 us (5%)
  between operations  0.77 us (2%)
    pallas_call x1, Pallas kernels, on_device(): pl.pallas_call(functools.partial(local_kernel, counts), out_shape=(jax.Sh...  11.7 us
    pallas_call x1, Pallas kernels, exchange(): pl.pallas_call(functools.partial(exchange_kernel, counts), out_shape=(jax...  11.3 us
    pallas_call x1, Pallas kernels, on_device(): pl.pallas_call(listed_kernel, out_shape=(jax.ShapeDtypeStruct((blocks, 8,...  8.73 us
    pallas_call x1, Pallas kernels, on_device(): pl.pallas_call(functools.partial(fluid_kernel, tile, gx_count), out_shape...  8.58 us
    pallas_call x1, Pallas kernels, on_device(): pl.pallas_call(final_kernel, out_shape=(jax.ShapeDtypeStruct((3, blocks,...  3.15 us
    unnamed x16, local copies, waits for them, and re-layouts  2.21 us
    pallas_call x1, Pallas kernels, on_device(): pl.pallas_call(state_kernel, out_shape=(jax.ShapeDtypeStruct((blocks, 8,...  1.1 us

profile of v3, /device:TPU:0, one launch (start us, length us, event | category | flops | bytes accessed | tf_op | source)
XLA Modules:
  0.0 50.2 jit_solution(12592068499485771559)
XLA Ops:
  0.6 0.0 copy-start.6
  0.6 0.0 copy-start.7
  0.7 0.0 copy-start
  0.7 0.7 %add_bitcast_fusion = s32[64]{0:T(128)S(1)} fusion(s32[1,64]{1,0:T(1,128)} %param.16), kind=kLoop, calls=%fused_computation.11 | loop fusion | flops 64 | bytes 512 | tf_op jit(solution)/shard_map/jit(_where)/broadcast_in_dim | solution.py:332
  1.4 0.7 %and_select_fusion = s32[64]{0:T(128)S(1)} fusion(s32[1,64,1]{1,2,0:T(1,128)} %param.14, s32[]{:T(128)S(6)} %add.60), kind=kLoop, calls=%fused_computation.9 | loop fusion | flops 768 | bytes 516 | tf_op jit(solution)/shard_map/jit(remainder)/select_n | solution.py:327
  2.0 0.2 convert_reduce_fusion
  2.2 0.0 copy-done.7
  2.2 0.1 select_reduce_fusion
  2.3 0.1 sub.7
  2.4 0.0 copy-done.6
  2.4 0.7 %pad_maximum_fusion.gy_ref = f32[6,16,128]{2,1,0:T(8,128)S(1)} fusion(f32[3,16,128]{2,1,0:T(8,128)S(1)} %bitcast.33, f32[3,16,128]{2,1,0:T(8,128)} %bitcast.34), kind=kLoop, calls=%fused_computation | loop fusion | flops 12288 | bytes 98304 | tf_op jit(solution)/shard_map/concatenate | solution.py:338
  3.2 0.0 copy-start.1
  3.2 0.0 copy-start.3
  3.2 11.3 %exchange.1 = (s32[8,1,128]{2,1,0:T(1,128)S(1)}, f32[4,6,16,128]{3,2,1,0:T(8,128)S(1)}) custom-call(s32[8,1,128]{2,1,0:T(1,128)S(1)} %pad.4.gx_ref, f32[6,16,128]{2,1,0:T(8,128)S(1)} %pad_maximum_fusion.gy_ref), custom_call_target="tpu_custom_call" | custom-call | tf_op jit(solution)/shard_map/exchange/pallas_call | solution.py:75
  14.6 0.1 reshape_squeeze.3.asked_ref
  14.6 0.0 copy-done
  14.6 0.0 copy-done.1
  14.6 0.0 copy-done.3
  14.7 0.0 copy-start.2
  14.7 0.9 %copy-done.2 = f32[3,1,8192]{2,1,0:T(1,128)S(1)} copy-done((f32[3,1,8192]{2,1,0:T(1,128)S(1)}, f32[3,1,8192]{2,1,0:T(1,128)}, u32[]{:S(2)}) %copy-start.2) | copy-done | bytes 98328
  15.6 1.1 %states.1 = (f32[64,8,128]{2,1,0:T(8,128)S(1)}, f32[128,8,128]{2,1,0:T(8,128)S(1)}) custom-call(s32[128]{0:T(128)S(1)} %reshape_squeeze.3.asked_ref, f32[3,64,128]{2,1,0:T(8,128)S(1)} %bitcast.28, f32[3,64,128]{2,1,0:T(8,128)S(1)} %bitcast.22, f32[64,128]{1,0:T(8,128)S(1)} %bitcast.26, s32[64,128]{1,0:T(8,128)S(1)} %bitcast.30), custom_call_target="tpu_custom_call" | custom-call | tf_op jit(solution)/shard_map/states/pallas_call | solution.py:342
  16.7 0.0 copy-start.5
  16.7 0.6 %copy-done.5 = s32[1,4]{1,0:T(1,128)S(1)} copy-done((s32[1,4]{1,0:T(1,128)S(1)}, s32[1,4]{1,0:T(1,128)}, u32[]{:S(2)}) %copy-start.5) | copy-done | bytes 40
  17.3 8.6 %fluid.1 = (f32[3,1,8192]{2,1,0:T(1,128)S(1)}, f32[4,3,16,128]{3,2,1,0:T(8,128)S(1)}, f32[8,128,128]{2,1,0:T(8,128)S(1)}) custom-call(s32[1,4]{1,0:T(1,128)S(1)} %copy-done.5, s32[1,8192]{1,0:T(1,128)S(1)} %copy-done.3, f32[3,1,8192]{2,1,0:T(1,128)S(1)} %copy-done, f32[1,8192]{1,0:T(1,128)S(1)} %copy-done.1, ...), custom_call_target="tpu_custom_call" | custom-call | flops 4000000000 | bytes 1000000 | tf_op jit(solution)/shard_map/fluid/pallas_call | solution.py:360
  25.9 0.0 copy-start.4
  25.9 0.6 %copy-done.4 = s32[1,64]{1,0:T(1,128)S(1)} copy-done((s32[1,64]{1,0:T(1,128)S(1)}, s32[1,64]{1,0:T(1,128)}, u32[]{:S(2)}) %copy-start.4) | copy-done | bytes 280
  26.6 8.7 %listed.1 = (f32[64,8,128]{2,1,0:T(8,128)S(1)}, f32[512,128]{1,0:T(8,128)S(1)}) custom-call(s32[64]{0:T(128)S(1)} %bitcast.31, s32[64]{0:T(128)S(1)} %multiply_add_fusion.slot_ref, f32[64,8,128]{2,1,0:T(8,128)S(1)} %get-tuple-element.17.state_ref, f32[128,8,128]{2,1,0:T(8,128)S(1)} %bitcast.21), custom_call_target="tpu_custom_call" | custom-call | tf_op jit(solution)/shard_map/listed/pallas_call | solution.py:389
  35.3 11.7 %local.1 = (f32[64,8,128]{2,1,0:T(8,128)S(1)}, f32[8,64,128]{2,1,0:T(8,128)S(1)}, f32[4,3,16,128]{3,2,1,0:T(8,128)S(1)}) custom-call(f32[64,8,128]{2,1,0:T(8,128)S(1)} %get-tuple-element.17.state_ref, f32[64,8,128]{2,1,0:T(8,128)S(1)} %get-tuple-element.21.listed_ref, f32[8,64,128]{2,1,0:T(8,128)S(1)} %bitcast.24, f32[4,3,16,128]{3,2,1,0:T(8,128)S(1)} %get-tuple-element.23.gy_ref), custom_call_target="tpu_custom_call" | custom-call | tf_op jit(solution)/shard_map/local/pallas_call | solution.py:400
  47.1 3.1 %final.1 = (f32[3,64,128]{2,1,0:T(8,128)}, f32[3,16,128]{2,1,0:T(8,128)}) custom-call(s32[128]{0:T(128)S(1)} %reshape_squeeze.3.asked_ref, f32[64,8,128]{2,1,0:T(8,128)S(1)} %get-tuple-element.24.acc_ref, f32[512,128]{1,0:T(8,128)S(1)} %bitcast.25, f32[64,8,128]{2,1,0:T(8,128)S(1)} %get-tuple-element.17.state_ref, f32[3,64,128]{2,1,0:T(8,128)S(1)} %bitcast.29, ...), custom_call_target="tpu_custom_call" | custom-call | tf_op jit(solution)/shard_map/final/pallas_call | solution.py:418
  (4 shorter events, 0.0 us)
Async XLA Ops:
  0.6 1.8 %copy-start.6 = (f32[3,1,2048]{2,1,0:T(1,128)S(1)}, f32[3,1,2048]{2,1,0:T(1,128)}, u32[]{:S(2)}) copy-start(f32[3,1,2048]{2,1,0:T(1,128)} %param.19) | copy-start | bytes 73732
  0.6 1.6 %copy-start.7 = (s32[1,64,1]{1,2,0:T(1,128)S(1)}, s32[1,64,1]{1,2,0:T(1,128)}, u32[]{:S(2)}) copy-start(s32[1,64,1]{1,2,0:T(1,128)} %param.14) | copy-start | bytes 772
  0.7 14.0 %copy-start = (f32[3,1,8192]{2,1,0:T(1,128)S(1)}, f32[3,1,8192]{2,1,0:T(1,128)}, u32[]{:S(2)}) copy-start(f32[3,1,8192]{2,1,0:T(1,128)} %speed_ref.1) | copy-start | bytes 294916
  3.2 11.5 %copy-start.1 = (f32[1,8192]{1,0:T(1,128)S(1)}, f32[1,8192]{1,0:T(1,128)}, u32[]{:S(2)}) copy-start(f32[1,8192]{1,0:T(1,128)} %radius_ref.1) | copy-start | bytes 98308
  3.2 11.5 %copy-start.3 = (s32[1,8192]{1,0:T(1,128)S(1)}, s32[1,8192]{1,0:T(1,128)}, u32[]{:S(2)}) copy-start(s32[1,8192]{1,0:T(1,128)} %cell_ref.1) | copy-start | bytes 98308
  14.7 0.9 %copy-start.2 = (f32[3,1,8192]{2,1,0:T(1,128)S(1)}, f32[3,1,8192]{2,1,0:T(1,128)}, u32[]{:S(2)}) copy-start(f32[3,1,8192]{2,1,0:T(1,128)} %param.10) | copy-start | bytes 294916
  16.7 0.7 %copy-start.5 = (s32[1,4]{1,0:T(1,128)S(1)}, s32[1,4]{1,0:T(1,128)}, u32[]{:S(2)}) copy-start(s32[1,4]{1,0:T(1,128)} %owner_ref.1) | copy-start | bytes 52
  25.9 0.7 %copy-start.4 = (s32[1,64]{1,0:T(1,128)S(1)}, s32[1,64]{1,0:T(1,128)}, u32[]{:S(2)}) copy-start(s32[1,64]{1,0:T(1,128)} %param.15) | copy-start | bytes 772
